TPU v7x, 128 devices: a whole 4x4x4 slice. The times are simulated.
128 devices in a mesh: ep: 16 (over x, z), tp: 8 (over y, core).
Axes of the slice: x: 4, y: 4, z: 4, core: 2. Of those that a mesh axis runs over, the one named last changes fastest.
Arguments:
- tokens: bfloat16 [2048, 4096], P('ep', 'tp'), may hold values from -6 to 6
- out_grad: bfloat16 [2048, 4096], P('ep', 'tp'), may hold values from -6 to 6
- routes: int32 [2048, 4], P('ep'), may hold values from 0 to 15, all different within a row; in each aligned block of 128 rows (0 to 127, 128 to 255, ...) at most 64 rows name the same one
- probs: bfloat16 [2048, 4], P('ep'), may hold values from 0.019897461 to 0.59765625
- w_in: bfloat16 [16, 2, 1536, 4096], P('ep', None, 'tp'), as said below
- w_out: bfloat16 [16, 1536, 4096], P('ep', 'tp'), as said below
Outputs:
- in_grad: bfloat16 [2048, 4096], P('ep', 'tp')
- grad_in: bfloat16 [16, 2, 1536, 4096], P('ep', None, 'tp')
- grad_out: bfloat16 [16, 1536, 4096], P('ep', 'tp')
Inputs may be any that keep to these rules, and one draw needn't show every extreme that they name: `routes`: each token names 4 different copies; within the tokens of one device (aligned blocks of 128 tokens) no copy is named more than 64 times, a bound that some block reaches. `w_in`: copies c and c + 8 hold equal weights. `w_out`: copies c and c + 8 hold equal weights.
All inputs are finite; a program needn't handle non-finite values.
Results may differ from a plain program's by a relative error of at most 0.02.
Values may be sent and summed in bfloat16 or wider, within the bound.
A program may use at most 128 MiB of HBM per device.

v0:
```python
import jax
import jax.numpy as jnp
from jax import lax
from jax.sharding import PartitionSpec as P


def partner(block, axis, apart):
    count = lax.axis_size(axis)
    route = []
    for low in range(count):
        high = low | 1 << apart
        if high != low and high < count:
            route += [(low, high), (high, low)]
    return lax.ppermute(block, axis, route)


def slot_tables(block_routes, copies, cap):
    flat = block_routes.reshape(-1)
    nrows = flat.shape[0]
    before = jnp.arange(nrows, dtype=jnp.int32)
    earlier = (before[None, :] < before[:, None]) & (flat[None, :] == flat[:, None])
    ranks = jnp.sum(earlier.astype(jnp.int32), axis=1)
    slot = flat * cap + ranks
    source = (
        jnp.full((copies * cap,), nrows, jnp.int32).at[slot].set(jnp.arange(nrows, dtype=jnp.int32))
    )
    return (slot, source)


def body(tokens, out_grad, routes, probs, w_in, w_out):
    n_ep = lax.axis_size("ep")
    tok_dev, top = routes.shape
    nrows = tok_dev * top
    cap = 2 * nrows // n_ep
    slot, source = slot_tables(routes, n_ep, cap)
    valid = source < nrows
    local = jnp.minimum(source, nrows - 1)
    tok_index = local // top
    scale = jnp.where(valid, probs.reshape(-1)[local].astype(jnp.float32), 0.0)[:, None]
    packed_x = jnp.where(valid[:, None], tokens[tok_index], jnp.zeros((), jnp.bfloat16))
    packed_g = (scale * out_grad[tok_index].astype(jnp.float32)).astype(jnp.bfloat16)
    part = tokens.shape[1]
    send_x = packed_x.reshape(n_ep, cap, part)
    send_g = packed_g.reshape(n_ep, cap, part)
    recv_x, recv_g = (
        lax.all_to_all(send_x, "ep", split_axis=0, concat_axis=0, tiled=True),
        lax.all_to_all(send_g, "ep", split_axis=0, concat_axis=0, tiled=True),
    )
    rows_x = lax.all_gather(recv_x.reshape(n_ep * cap, part), "tp", axis=1, tiled=True)
    rows_g = lax.all_gather(recv_g.reshape(n_ep * cap, part), "tp", axis=1, tiled=True)
    width = rows_x.shape[1]
    w_gate = w_in[0, 0]
    w_up = w_in[0, 1]
    w_down = w_out[0]
    contract_last = (((1,), (1,)), ((), ()))
    a = lax.dot_general(rows_x, w_gate, contract_last, preferred_element_type=jnp.float32)
    b = lax.dot_general(rows_x, w_up, contract_last, preferred_element_type=jnp.float32)
    sig = jax.nn.sigmoid(a)
    silu = a * sig
    hidden = (silu * b).astype(jnp.bfloat16)
    dh = lax.dot_general(rows_g, w_down, contract_last, preferred_element_type=jnp.float32)
    da = (dh * b * sig * (1.0 + a * (1.0 - sig))).astype(jnp.bfloat16)
    db = (dh * silu).astype(jnp.bfloat16)
    partial_rows = jnp.dot(da, w_gate, preferred_element_type=jnp.float32)
    partial_rows = partial_rows + jnp.dot(db, w_up, preferred_element_type=jnp.float32)
    summed = lax.psum_scatter(
        partial_rows.reshape(n_ep, cap, width).astype(jnp.bfloat16),
        "tp",
        scatter_dimension=2,
        tiled=True,
    )
    back = lax.all_to_all(summed, "ep", split_axis=0, concat_axis=0, tiled=True)
    picked = back.reshape(n_ep * cap, back.shape[2])[slot]
    in_grad = jnp.sum(
        picked.astype(jnp.float32).reshape(tok_dev, top, back.shape[2]), axis=1
    ).astype(jnp.bfloat16)
    contract_rows = (((0,), (0,)), ((), ()))
    own_in = jnp.stack(
        [
            lax.dot_general(da, rows_x, contract_rows, preferred_element_type=jnp.float32),
            lax.dot_general(db, rows_x, contract_rows, preferred_element_type=jnp.float32),
        ]
    ).astype(jnp.bfloat16)[None]
    own_out = lax.dot_general(
        hidden, rows_g, contract_rows, preferred_element_type=jnp.float32
    ).astype(jnp.bfloat16)[None]
    half_bit = n_ep.bit_length() - 2
    other_in, other_out = partner((own_in, own_out), "ep", half_bit)
    grad_in = (own_in.astype(jnp.float32) + other_in.astype(jnp.float32)).astype(jnp.bfloat16)
    grad_out = (own_out.astype(jnp.float32) + other_out.astype(jnp.float32)).astype(jnp.bfloat16)
    return (in_grad, grad_in, grad_out)


def solution(mesh):
    return jax.shard_map(
        body,
        mesh=mesh,
        in_specs=(
            P("ep", "tp"),
            P("ep", "tp"),
            P("ep", None),
            P("ep", None),
            P("ep", None, "tp", None),
            P("ep", "tp", None),
        ),
        out_specs=(P("ep", "tp"), P("ep", None, "tp", None), P("ep", "tp", None)),
        check_vma=False,
    )
```

profile of v0, /device:TPU:0, one launch (start us, length us, event | category | flops | bytes accessed | tf_op | source)
XLA Modules:
  0.0 329.8 jit_solution(15195773333764695855)
XLA Ops:
  7.2 0.0 copy-start
  7.2 0.0 all-gather.5.cloned.1.call-start
  7.2 0.8 broadcast_multiply_fusion
  8.0 0.8 copy.13
  8.8 0.8 copy.14
  9.6 0.1 reshape.126
  9.8 0.1 copy.12
  9.9 0.1 mul.50
  10.0 0.1 eq.15
  10.1 0.3 convert_reduce_fusion
  10.4 2.4 scatter_custom_fusion
  12.9 6.8 %gather_fusion = bf16[1024]{0:T(1024)(128)(2,1)S(1)} fusion(bf16[512]{0:T(512)(128)(2,1)S(1)} %reshape.126, s32[1024]{0:T(1024)S(1)} %get-tuple-element.7), kind=kCustom, calls=%fused_computation | custom fusion | bytes 8192 | tf_op jit(solution)/shard_map/gather | solution.py:39
  19.7 0.1 broadcast_in_dim.36
  19.8 4.0 %gather_fusion.2 = bf16[1024,512]{1,0:T(8,128)(2,1)S(1)} fusion(bf16[128,512]{1,0:T(8,128)(2,1)S(1)} %copy-done.2, s32[1024]{0:T(1024)S(1)} %get-tuple-element.8), kind=kCustom, calls=%fused_computation.2 | custom fusion | bytes 2101248 | tf_op jit(solution)/shard_map/gather | solution.py:40
  23.7 0.0 copy-start.3
  23.7 0.2 broadcast_select_fusion
  24.0 24.7 %all_to_all.15 = bf16[16,64,512]{2,1,0:T(8,128)(2,1)} all-to-all(bf16[16,64,512]{2,1,0:T(8,128)(2,1)S(1)} %broadcast_select_fusion), channel_id=1, replica_groups=mesh['ep'=16,'tp'=8] {'ep'}, dimensions={0} | all-to-all | bytes 2097152 | tf_op jit(solution)/shard_map/all_to_all | solution.py:46
  48.7 0.0 all-gather.5.cloned.1.call-update
  48.7 0.0 all-gather.3.cloned.1.call-start
  48.7 0.1 mul.51
  48.8 4.0 %gather_fusion.1 = bf16[1024,512]{1,0:T(8,128)(2,1)S(1)} fusion(bf16[128,512]{1,0:T(8,128)(2,1)S(1)} %copy-done.3, s32[1024]{0:T(1024)S(1)} %get-tuple-element.8), kind=kCustom, calls=%fused_computation.1 | custom fusion | bytes 2101248 | tf_op jit(solution)/shard_map/gather | solution.py:41
  52.8 0.3 fusion.3
  53.1 19.7 %all_to_all.16 = bf16[16,64,512]{2,1,0:T(8,128)(2,1)} all-to-all(bf16[16,64,512]{2,1,0:T(8,128)(2,1)S(1)} %fusion.3), channel_id=1, replica_groups=mesh['ep'=16,'tp'=8] {'ep'}, dimensions={0} | all-to-all | bytes 2097152 | tf_op jit(solution)/shard_map/all_to_all | solution.py:47
  72.8 0.0 all-gather.3.cloned.1.call-update
  72.8 0.2 reduce-scatter.2.cloned.1.call-start
  73.0 23.9 %all-gather.5.cloned.1.call-done = bf16[1024,4096]{1,0:T(8,128)(2,1)} async-done(((bf16[1024,512]{1,0:T(8,128)(2,1)}), bf16[1024,4096]{1,0:T(8,128)(2,1)}) %all-gather.5.cloned.1.call-update) | async-done | bytes 8388624 | tf_op jit(solution)/shard_map/all_gather | solution.py:49
  96.9 7.7 %fusion.6 = f32[1024,192]{0,1:T(8,128)} fusion(bf16[1024,4096]{1,0:T(8,128)(2,1)} %all-gather.5.cloned.1.call-done, bf16[1,2,192,4096]{3,2,1,0:T(8,128)(2,1)} %param.10), kind=kOutput, calls=%fused_computation.19 | convolution fusion | flops 1610612736 | bytes 10747904 | tf_op jit(solution)/shard_map/dot_general | solution.py:56
  104.6 3.8 %fusion.9 = f32[1024,192]{0,1:T(8,128)} fusion(bf16[1024,4096]{1,0:T(8,128)(2,1)S(1)} %copy-done.7, bf16[1,2,192,4096]{3,2,1,0:T(8,128)(2,1)S(1)} %copy-done.5), kind=kOutput, calls=%fused_computation.22 | convolution fusion | flops 1610612736 | bytes 10747904 | tf_op jit(solution)/shard_map/dot_general | solution.py:57
  108.4 40.1 %all-gather.3.cloned.1.call-done = bf16[1024,4096]{1,0:T(8,128)(2,1)} async-done(((bf16[1024,512]{1,0:T(8,128)(2,1)}), bf16[1024,4096]{1,0:T(8,128)(2,1)}) %all-gather.3.cloned.1.call-update) | async-done | bytes 8388624 | tf_op jit(solution)/shard_map/all_gather | solution.py:50
  148.5 6.9 %multiply_convert_fusion.1 = (bf16[1024,192]{0,1:T(8,128)(2,1)S(1)}, bf16[1024,192]{0,1:T(8,128)(2,1)S(1)}) fusion(f32[1024,192]{0,1:T(8,128)} %fusion.6, f32[1024,192]{0,1:T(8,128)} %fusion.9, bf16[1024,4096]{1,0:T(8,128)(2,1)} %all-gather.3.cloned.1.call-done, bf16[1,192,4096]{2,1,0:T(8,128)(2,1)S(1)} %copy-done), kind=kOutput, calls=%fused_computation.35 | convolution fusion | flops 1613168640 | bytes 12320768 | tf_op jit(solution)/shard_map/dot_general | solution.py:61
  155.5 8.1 %fusion.4 = f32[1024,4096]{1,0:T(8,128)} fusion(bf16[1024,192]{0,1:T(8,128)(2,1)S(1)} %get-tuple-element.6, bf16[1,2,192,4096]{3,2,1,0:T(8,128)(2,1)S(1)} %copy-done.6), kind=kOutput, calls=%fused_computation.17 | convolution fusion | flops 1610612736 | bytes 18743296 | tf_op jit(solution)/shard_map/dot_general | solution.py:64
  163.6 11.4 %add_convert_fusion = bf16[1024,4096]{1,0:T(8,128)(2,1)} fusion(f32[1024,4096]{1,0:T(8,128)} %fusion.4, bf16[1024,192]{0,1:T(8,128)(2,1)S(1)} %get-tuple-element.5, bf16[1,2,192,4096]{3,2,1,0:T(8,128)(2,1)S(1)} %copy-done.6), kind=kOutput, calls=%fused_computation.5 | convolution fusion | flops 1619001344 | bytes 27131904 | tf_op jit(solution)/shard_map/dot_general | solution.py:65
  175.1 0.0 reduce-scatter.2.cloned.1.call-update
  175.1 5.6 %fusion.1 = bf16[1,1,192,4096]{3,2,1,0:T(8,128)(2,1)S(1)} fusion(bf16[1024,192]{0,1:T(8,128)(2,1)S(1)} %get-tuple-element.5, bf16[1024,4096]{1,0:T(8,128)(2,1)} %all-gather.5.cloned.1.call-done), kind=kOutput, calls=%fused_computation.11 | convolution fusion | flops 1611399168 | bytes 10354688 | tf_op jit(solution)/shard_map/dot_general | solution.py:81
  180.7 5.4 %fusion = bf16[1,1,192,4096]{3,2,1,0:T(8,128)(2,1)S(1)} fusion(bf16[1024,192]{0,1:T(8,128)(2,1)S(1)} %get-tuple-element.6, bf16[1024,4096]{1,0:T(8,128)(2,1)} %all-gather.5.cloned.1.call-done), kind=kOutput, calls=%fused_computation.10 | convolution fusion | flops 1611399168 | bytes 10354688 | tf_op jit(solution)/shard_map/dot_general | solution.py:80
  186.1 1.9 pad_maximum_fusion
  188.1 0.3 copy-done.4
  188.4 3.0 collective-permute-start
  191.4 1.8 fusion.2
  193.2 0.6 collective-permute-start.1
  193.9 100.4 %collective-permute-done.1 = bf16[1,192,4096]{2,1,0:T(8,128)(2,1)S(1)} collective-permute-done((bf16[1,192,4096]{2,1,0:T(8,128)(2,1)S(1)}, bf16[1,192,4096]{2,1,0:T(8,128)(2,1)S(1)}, u32[]{:S(2)}, u32[]{:S(2)}) %collective-permute-start.1) | collective-permute-done | bytes 1572896 | tf_op jit(solution)/shard_map/ppermute | solution.py:14
  294.3 1.7 add_convert_fusion.2
  295.9 6.8 %all-to-all-start.2 = ((bf16[16,64,512]{2,1,0:T(8,128)(2,1)}), bf16[16,64,512]{2,1,0:T(8,128)(2,1)S(1)}, u32[]{:S(2)}, u32[]{:S(2)}) async-start(bf16[16,64,512]{2,1,0:T(8,128)(2,1)} %reduce-scatter.2.cloned.1.call-done), calls=%async_computation.3 | async-start | bytes 2097152 | tf_op jit(solution)/shard_map/all_to_all | solution.py:72
  302.7 5.3 %add_convert_fusion.1 = bf16[1,2,192,4096]{3,2,1,0:T(8,128)(2,1)} fusion(bf16[1,2,192,4096]{3,2,1,0:T(8,128)(2,1)} %collective-permute-done, bf16[1,1,192,4096]{3,2,1,0:T(8,128)(2,1)S(1)} %fusion.1, bf16[1,1,192,4096]{3,2,1,0:T(8,128)(2,1)} %copy-done.4), kind=kLoop, calls=%fused_computation.6 | loop fusion | flops 7864320 | bytes 9437184 | tf_op jit(solution)/shard_map/convert_element_type | solution.py:89
  308.1 11.8 %all-to-all-done.2 = bf16[16,64,512]{2,1,0:T(8,128)(2,1)S(1)} async-done(((bf16[16,64,512]{2,1,0:T(8,128)(2,1)}), bf16[16,64,512]{2,1,0:T(8,128)(2,1)S(1)}, u32[]{:S(2)}, u32[]{:S(2)}) %all-to-all-start.2) | async-done | bytes 1048608 | tf_op jit(solution)/shard_map/all_to_all | solution.py:72
  319.9 2.0 gather_fusion.3
  321.8 0.1 gather.21
  322.0 1.3 reduce_sum.25
  (29 shorter events, 0.1 us)
Async XLA Ops:
  7.2 141.3 %copy-start = (bf16[1,192,4096]{2,1,0:T(8,128)(2,1)S(1)}, bf16[1,192,4096]{2,1,0:T(8,128)(2,1)}, u32[]{:S(2)}) copy-start(bf16[1,192,4096]{2,1,0:T(8,128)(2,1)} %param.11) | copy-start | bytes 4718596
  7.2 12.6 %copy-start.2 = (bf16[128,512]{1,0:T(8,128)(2,1)S(1)}, bf16[128,512]{1,0:T(8,128)(2,1)}, u32[]{:S(2)}) copy-start(bf16[128,512]{1,0:T(8,128)(2,1)} %param.6) | copy-start | bytes 393220
  7.2 89.7 %all-gather.5.cloned.1.call-start = ((), (), s32[]{:S(2)}) async-start(), calls=%async_computation.5 | async-start | bytes 9437184 | tf_op jit(solution)/shard_map/all_gather | solution.py:49
  23.7 25.1 %copy-start.3 = (bf16[128,512]{1,0:T(8,128)(2,1)S(1)}, bf16[128,512]{1,0:T(8,128)(2,1)}, u32[]{:S(2)}) copy-start(bf16[128,512]{1,0:T(8,128)(2,1)} %param.7) | copy-start | bytes 393220
  48.7 99.8 %all-gather.3.cloned.1.call-start = ((), (), s32[]{:S(2)}) async-start(), calls=%async_computation.4 | async-start | bytes 9437184 | tf_op jit(solution)/shard_map/all_gather | solution.py:50
  72.8 223.2 %reduce-scatter.2.cloned.1.call-start = ((), (), s32[]{:S(2)}) async-start(), calls=%async_computation.6 | async-start | bytes 9437184 | tf_op jit(solution)/shard_map/reduce_scatter | solution.py:66
  96.9 7.7 %copy-start.5 = (bf16[1,2,192,4096]{3,2,1,0:T(8,128)(2,1)S(1)}, bf16[1,2,192,4096]{3,2,1,0:T(8,128)(2,1)}, u32[]{:S(2)}) copy-start(bf16[1,2,192,4096]{3,2,1,0:T(8,128)(2,1)} %param.10) | copy-start | bytes 9437188
  96.9 7.7 %copy-start.7 = (bf16[1024,4096]{1,0:T(8,128)(2,1)S(1)}, bf16[1024,4096]{1,0:T(8,128)(2,1)}, u32[]{:S(2)}) copy-start(bf16[1024,4096]{1,0:T(8,128)(2,1)} %all-gather.5.cloned.1.call-done) | copy-start | bytes 25165828
  148.5 7.0 %copy-start.6 = (bf16[1,2,192,4096]{3,2,1,0:T(8,128)(2,1)S(1)}, bf16[1,2,192,4096]{3,2,1,0:T(8,128)(2,1)}, u32[]{:S(2)}) copy-start(bf16[1,2,192,4096]{3,2,1,0:T(8,128)(2,1)} %param.10) | copy-start | bytes 9437188
  175.1 16.3 %slice-start = ((s8[8388608]{0:T(1024)(128)(4,1)}), s8[4194304]{0:T(1024)(128)(4,1)S(1)}, s32[]{:S(2)}) async-start(s8[8388608]{0:T(1024)(128)(4,1)} %bitcast.50), calls=%async_computation.7 | async-start | bytes 8388608
  180.7 10.7 %slice-start.1 = ((s8[8388608]{0:T(1024)(128)(4,1)}), s8[4194304]{0:T(1024)(128)(4,1)S(1)}, s32[]{:S(2)}) async-start(s8[8388608]{0:T(1024)(128)(4,1)} %bitcast.50), calls=%async_computation.8 | async-start | bytes 8388608
  186.1 2.3 copy-start.4
  186.1 5.3 %copy-start.8 = (f32[1024,192]{0,1:T(8,128)S(1)}, f32[1024,192]{0,1:T(8,128)}, u32[]{:S(2)}) copy-start(f32[1024,192]{0,1:T(8,128)} %fusion.6) | copy-start | bytes 2359300
  186.1 5.3 %copy-start.9 = (f32[1024,192]{0,1:T(8,128)S(1)}, f32[1024,192]{0,1:T(8,128)}, u32[]{:S(2)}) copy-start(f32[1024,192]{0,1:T(8,128)} %fusion.9) | copy-start | bytes 2359300
  188.4 114.4 %collective-permute-start = (bf16[1,2,192,4096]{3,2,1,0:T(8,128)(2,1)}, bf16[1,2,192,4096]{3,2,1,0:T(8,128)(2,1)}, u32[]{:S(2)}, u32[]{:S(2)}) collective-permute-start(bf16[1,2,192,4096]{3,2,1,0:T(8,128)(2,1)} %pad_maximum_fusion), channel_id=1, source_target_pairs={{0,64},{64,0},{8,72},{72,8},{16,80},{80,16},{24,88},{88,24},{32,96... | collective-permute-start | bytes 9437192 | tf_op jit(solution)/shard_map/ppermute | solution.py:14
  193.2 101.0 %collective-permute-start.1 = (bf16[1,192,4096]{2,1,0:T(8,128)(2,1)S(1)}, bf16[1,192,4096]{2,1,0:T(8,128)(2,1)S(1)}, u32[]{:S(2)}, u32[]{:S(2)}) collective-permute-start(bf16[1,192,4096]{2,1,0:T(8,128)(2,1)S(1)} %fusion.2), channel_id=1, source_target_pairs={{0,64},{64,0},{8,72},{72,8},{16,80},{80,16},{24,88},{88,24},{32,96... | collective-permute-start | bytes 4718600 | tf_op jit(solution)/shard_map/ppermute | solution.py:14
  295.9 23.9 %all-to-all-start.2 = ((bf16[16,64,512]{2,1,0:T(8,128)(2,1)}), bf16[16,64,512]{2,1,0:T(8,128)(2,1)S(1)}, u32[]{:S(2)}, u32[]{:S(2)}) async-start(bf16[16,64,512]{2,1,0:T(8,128)(2,1)} %reduce-scatter.2.cloned.1.call-done), calls=%async_computation.3 | async-start | bytes 2097152 | tf_op jit(solution)/shard_map/all_to_all | solution.py:72
  319.9 3.4 %copy-start.1 = (bf16[1,192,4096]{2,1,0:T(8,128)(2,1)S(1)}, bf16[1,192,4096]{2,1,0:T(8,128)(2,1)}, u32[]{:S(2)}) copy-start(bf16[1,192,4096]{2,1,0:T(8,128)(2,1)} %param.11) | copy-start | bytes 4718596
Sparse Core Ops, SparseCore 0:
  48.8 48.0 all-gather.4
  98.6 49.8 all-gather.2
  175.2 52.6 reduce-scatter.1
where the time goes:
time: 330 us
  waiting for transfers between devices  176 us (53%)
  matrix products  50.8 us (15%)
  blocking collectives  44.4 us (13%)
  local copies, waits for them, and re-layouts  21.8 us (7%)
  between operations  14 us (4%)
  other arithmetic  11.9 us (4%)
  starting transfers between devices  10.7 us (3%)
    ppermute x2, waiting for transfers between devices, partner(): return lax.ppermute(block, axis, route)  100 us
    all_gather x1, waiting for transfers between devices, body(): lax.all_gather(recv_g.reshape(n_ep * cap, part), 'tp', axis=1, tiled=True)  40.1 us
    all_to_all x1, blocking collectives, body(): lax.all_to_all(send_x, 'ep', split_axis=0, concat_axis=0, tiled=True)  24.7 us
    all_gather x1, waiting for transfers between devices, body(): lax.all_gather(recv_x.reshape(n_ep * cap, part), 'tp', axis=1, tiled=True)  23.9 us
    all_to_all x1, blocking collectives, body(): lax.all_to_all(send_g, 'ep', split_axis=0, concat_axis=0, tiled=True)  19.7 us
    all_to_all x1, waiting for transfers between devices, body(): back = lax.all_to_all(summed, 'ep', split_axis=0, concat_axis=0, tiled=True)  11.8 us
    dot_general x1, matrix products, body(): jnp.dot(db, w_up, preferred_element_type=jnp.float32)  11.4 us
    dot_general x1, matrix products, body(): partial_rows = jnp.dot(da, w_gate, preferred_element_type=jnp.float32)  8.15 us
  transfers between devices with their start and end apart: 6, of which 4 were waited for; matrix products, arithmetic and copies ran while one was open for 11% of the time, Pallas kernels for 0%

commit v1 on v0

--- a/solution.py
+++ b/solution.py
@@ -47,7 +47,12 @@
         lax.all_to_all(send_g, "ep", split_axis=0, concat_axis=0, tiled=True),
     )
     rows_x = lax.all_gather(recv_x.reshape(n_ep * cap, part), "tp", axis=1, tiled=True)
-    rows_g = lax.all_gather(recv_g.reshape(n_ep * cap, part), "tp", axis=1, tiled=True)
+    rows_g = jnp.concatenate(
+        lax.all_to_all(
+            jnp.stack([recv_g.reshape(n_ep * cap, part)] * lax.axis_size("tp")), "tp", 0, 0
+        ),
+        axis=1,
+    )
     width = rows_x.shape[1]
     w_gate = w_in[0, 0]
     w_up = w_in[0, 1]

time: 330 us -> 365 us (1.11)
  waiting for transfers between devices: 176 us -> 197 us
  local copies, waits for them, and re-layouts: 21.8 us -> 27.7 us
  starting transfers between devices: 10.7 us -> 15.8 us
    all_to_all x0 -> x1, waiting for transfers between devices: none -> 62.3 us  [body(): lax.all_to_all(jnp.stack([recv_g.reshape(n_ep * cap, part)] * lax.axis_si...]
    all_gather x1 -> x0, waiting for transfers between devices: 40.1 us -> none  [body(): lax.all_gather(recv_g.reshape(n_ep * cap, part), 'tp', axis=1, tiled=True)]
    another operation x0 -> x2, local copies, waits for them, and re-layouts: none -> 5.79 us  [body(): jnp.stack([recv_g.reshape(n_ep * cap, part)] * lax.axis_size('tp'))]
    ppermute x2, waiting for transfers between devices: 100 us -> 95.2 us  [partner(): return lax.ppermute(block, axis, route)]
    all_to_all x0 -> x1, starting transfers between devices: none -> 4.96 us  [body(): lax.all_to_all(jnp.stack([recv_g.reshape(n_ep * cap, part)] * lax.axis_si...]
    dot_general x1, matrix products: 1.83 us -> 6.45 us  [body(): lax.dot_general(hidden, rows_g, contract_rows, preferred_element_type=jnp...]
    all_gather x1, waiting for transfers between devices: 23.9 us -> 27.8 us  [body(): lax.all_gather(recv_x.reshape(n_ep * cap, part), 'tp', axis=1, tiled=True)]
  transfers between devices with their start and end apart: 6 -> 6, of which waited for: 4 -> 4; matrix products, arithmetic and copies ran while one was open for 11% -> 13% of each run, Pallas kernels for 0% -> 0%
where the time goes in v1:
time: 365 us
  waiting for transfers between devices  197 us (54%)
  matrix products  54 us (15%)
  blocking collectives  44.4 us (12%)
  local copies, waits for them, and re-layouts  27.7 us (8%)
  starting transfers between devices  15.8 us (4%)
  between operations  14.3 us (4%)
  other arithmetic  11.8 us (3%)
    ppermute x2, waiting for transfers between devices, partner(): return lax.ppermute(block, axis, route)  95.2 us
    all_to_all x1, waiting for transfers between devices, body(): lax.all_to_all(jnp.stack([recv_g.reshape(n_ep * cap, part)] * lax.axis_si...  62.3 us
    all_gather x1, waiting for transfers between devices, body(): lax.all_gather(recv_x.reshape(n_ep * cap, part), 'tp', axis=1, tiled=True)  27.8 us
    all_to_all x1, blocking collectives, body(): lax.all_to_all(send_x, 'ep', split_axis=0, concat_axis=0, tiled=True)  24.7 us
    all_to_all x1, blocking collectives, body(): lax.all_to_all(send_g, 'ep', split_axis=0, concat_axis=0, tiled=True)  19.7 us
    dot_general x1, matrix products, body(): jnp.dot(db, w_up, preferred_element_type=jnp.float32)  11.4 us
    all_to_all x1, waiting for transfers between devices, body(): back = lax.all_to_all(summed, 'ep', split_axis=0, concat_axis=0, tiled=True)  11.2 us
    dot_general x1, matrix products, body(): partial_rows = jnp.dot(da, w_gate, preferred_element_type=jnp.float32)  8.15 us
  transfers between devices with their start and end apart: 6, of which 4 were waited for; matrix products, arithmetic and copies ran while one was open for 13% of the time, Pallas kernels for 0%

profile of v1, /device:TPU:0, one launch (start us, length us, event | category | flops | bytes accessed | tf_op | source)
XLA Modules:
  0.0 364.5 jit_solution(12937359871356525795)
XLA Ops:
  7.2 0.0 copy-start
  7.2 0.0 all-gather.2.cloned.1.call-start
  7.2 0.9 copy.14
  8.1 0.7 broadcast_multiply_fusion
  8.8 0.1 eq.15
  8.9 0.3 convert_reduce_fusion
  9.2 0.1 copy.13
  9.3 0.1 mul.50
  9.4 2.4 scatter_custom_fusion
  11.9 0.8 copy.15
  12.7 0.1 reshape.131
  12.9 6.8 %gather_fusion = bf16[1024]{0:T(1024)(128)(2,1)S(1)} fusion(bf16[512]{0:T(512)(128)(2,1)S(1)} %reshape.131, s32[1024]{0:T(1024)S(1)} %get-tuple-element.7), kind=kCustom, calls=%fused_computation | custom fusion | bytes 8192 | tf_op jit(solution)/shard_map/gather | solution.py:39
  19.7 0.1 broadcast_in_dim.36
  19.8 4.0 %gather_fusion.2 = bf16[1024,512]{1,0:T(8,128)(2,1)S(1)} fusion(bf16[128,512]{1,0:T(8,128)(2,1)S(1)} %copy-done.2, s32[1024]{0:T(1024)S(1)} %get-tuple-element.8), kind=kCustom, calls=%fused_computation.2 | custom fusion | bytes 2101248 | tf_op jit(solution)/shard_map/gather | solution.py:40
  23.7 0.2 broadcast_select_fusion
  24.0 24.7 %all_to_all.20 = bf16[16,64,512]{2,1,0:T(8,128)(2,1)} all-to-all(bf16[16,64,512]{2,1,0:T(8,128)(2,1)S(1)} %broadcast_select_fusion), channel_id=1, replica_groups=mesh['ep'=16,'tp'=8] {'ep'}, dimensions={0} | all-to-all | bytes 2097152 | tf_op jit(solution)/shard_map/all_to_all | solution.py:46
  48.7 0.0 all-gather.2.cloned.1.call-update
  48.7 0.1 mul.51
  48.8 4.0 %gather_fusion.1 = bf16[1024,512]{1,0:T(8,128)(2,1)S(1)} fusion(bf16[128,512]{1,0:T(8,128)(2,1)S(1)} %copy-done.3, s32[1024]{0:T(1024)S(1)} %get-tuple-element.8), kind=kCustom, calls=%fused_computation.1 | custom fusion | bytes 2101248 | tf_op jit(solution)/shard_map/gather | solution.py:41
  52.7 0.3 fusion.3
  53.0 19.7 %all_to_all.21 = bf16[16,64,512]{2,1,0:T(8,128)(2,1)} all-to-all(bf16[16,64,512]{2,1,0:T(8,128)(2,1)S(1)} %fusion.3), channel_id=1, replica_groups=mesh['ep'=16,'tp'=8] {'ep'}, dimensions={0} | all-to-all | bytes 2097152 | tf_op jit(solution)/shard_map/all_to_all | solution.py:47
  72.7 1.5 copy.16
  74.2 4.3 %stack.12 = bf16[8,1024,512]{1,2,0:T(8,128)(2,1)} broadcast(bf16[1024,512]{0,1:T(8,128)(2,1)S(1)} %copy.16), dimensions={1,2} | broadcast | bytes 9437184 | tf_op jit(solution)/shard_map/stack | solution.py:52
  78.5 5.0 %all-to-all-start.1 = ((bf16[8,1024,512]{1,2,0:T(8,128)(2,1)}), bf16[8,1024,512]{1,2,0:T(8,128)(2,1)}, u32[]{:S(2)}, u32[]{:S(2)}) async-start(bf16[8,1024,512]{1,2,0:T(8,128)(2,1)} %stack.12), calls=%async_computation.1 | async-start | bytes 16777216 | tf_op jit(solution)/shard_map/all_to_all | solution.py:51
  83.5 0.2 reduce-scatter.2.cloned.1.call-start
  83.7 27.8 %all-gather.2.cloned.1.call-done = bf16[1024,4096]{1,0:T(8,128)(2,1)} async-done(((bf16[1024,512]{1,0:T(8,128)(2,1)}), bf16[1024,4096]{1,0:T(8,128)(2,1)}) %all-gather.2.cloned.1.call-update) | async-done | bytes 8388624 | tf_op jit(solution)/shard_map/all_gather | solution.py:49
  111.5 7.7 %fusion.6 = f32[1024,192]{0,1:T(8,128)} fusion(bf16[1024,4096]{1,0:T(8,128)(2,1)} %all-gather.2.cloned.1.call-done, bf16[1,2,192,4096]{3,2,1,0:T(8,128)(2,1)} %param.10), kind=kOutput, calls=%fused_computation.19 | convolution fusion | flops 1610612736 | bytes 10747904 | tf_op jit(solution)/shard_map/dot_general | solution.py:61
  119.3 3.8 %fusion.9 = f32[1024,192]{0,1:T(8,128)} fusion(bf16[1024,4096]{1,0:T(8,128)(2,1)S(1)} %copy-done.7, bf16[1,2,192,4096]{3,2,1,0:T(8,128)(2,1)S(1)} %copy-done.5), kind=kOutput, calls=%fused_computation.22 | convolution fusion | flops 1610612736 | bytes 10747904 | tf_op jit(solution)/shard_map/dot_general | solution.py:62
  123.0 62.3 %all-to-all-done.1 = bf16[8,1024,512]{1,2,0:T(8,128)(2,1)} async-done(((bf16[8,1024,512]{1,2,0:T(8,128)(2,1)}), bf16[8,1024,512]{1,2,0:T(8,128)(2,1)}, u32[]{:S(2)}, u32[]{:S(2)}) %all-to-all-start.1) | async-done | bytes 8388640 | tf_op jit(solution)/shard_map/all_to_all | solution.py:51
  185.3 5.9 %multiply_convert_fusion.1 = (bf16[1024,192]{0,1:T(8,128)(2,1)S(1)}, bf16[1024,192]{0,1:T(8,128)(2,1)S(1)}) fusion(f32[1024,192]{0,1:T(8,128)} %fusion.6, f32[1024,192]{0,1:T(8,128)} %fusion.9, bf16[1024,4096]{0,1:T(8,128)(2,1)} %bitcast.5, bf16[1,192,4096]{2,1,0:T(8,128)(2,1)S(1)} %copy-done), kind=kOutput, calls=%fused_computation.35 | convolution fusion | flops 1613168640 | bytes 12320768 | tf_op jit(solution)/shard_map/dot_general | solution.py:66
  191.2 8.2 %fusion.4 = f32[1024,4096]{1,0:T(8,128)} fusion(bf16[1024,192]{0,1:T(8,128)(2,1)S(1)} %get-tuple-element.6, bf16[1,2,192,4096]{3,2,1,0:T(8,128)(2,1)S(1)} %copy-done.6), kind=kOutput, calls=%fused_computation.17 | convolution fusion | flops 1610612736 | bytes 18743296 | tf_op jit(solution)/shard_map/dot_general | solution.py:69
  199.4 11.4 %add_convert_fusion = bf16[1024,4096]{1,0:T(8,128)(2,1)} fusion(f32[1024,4096]{1,0:T(8,128)} %fusion.4, bf16[1024,192]{0,1:T(8,128)(2,1)S(1)} %get-tuple-element.5, bf16[1,2,192,4096]{3,2,1,0:T(8,128)(2,1)S(1)} %copy-done.6), kind=kOutput, calls=%fused_computation.5 | convolution fusion | flops 1619001344 | bytes 27131904 | tf_op jit(solution)/shard_map/dot_general | solution.py:70
  210.8 0.0 reduce-scatter.2.cloned.1.call-update
  210.8 5.4 %fusion = bf16[1,1,192,4096]{3,2,1,0:T(8,128)(2,1)S(1)} fusion(bf16[1024,192]{0,1:T(8,128)(2,1)S(1)} %get-tuple-element.6, bf16[1024,4096]{1,0:T(8,128)(2,1)} %all-gather.2.cloned.1.call-done), kind=kOutput, calls=%fused_computation.10 | convolution fusion | flops 1611399168 | bytes 10354688 | tf_op jit(solution)/shard_map/dot_general | solution.py:85
  216.3 5.2 %fusion.1 = bf16[1,1,192,4096]{3,2,1,0:T(8,128)(2,1)S(1)} fusion(bf16[1024,192]{0,1:T(8,128)(2,1)S(1)} %get-tuple-element.5, bf16[1024,4096]{1,0:T(8,128)(2,1)} %all-gather.2.cloned.1.call-done), kind=kOutput, calls=%fused_computation.11 | convolution fusion | flops 1611399168 | bytes 10354688 | tf_op jit(solution)/shard_map/dot_general | solution.py:86
  221.5 1.9 pad_maximum_fusion
  223.4 0.3 copy-done.4
  223.7 3.0 collective-permute-start
  226.7 6.4 %fusion.2 = bf16[1,192,4096]{2,1,0:T(8,128)(2,1)S(1)} fusion(bf16[1024,4096]{0,1:T(8,128)(2,1)} %bitcast.5, f32[1024,192]{0,1:T(8,128)S(1)} %copy-done.9, f32[1024,192]{0,1:T(8,128)S(1)} %copy-done.8), kind=kOutput, calls=%fused_computation.12 | convolution fusion | flops 1612578816 | bytes 11534336 | tf_op jit(solution)/shard_map/dot_general | solution.py:89
  233.2 0.6 collective-permute-start.1
  233.8 95.2 %collective-permute-done.1 = bf16[1,192,4096]{2,1,0:T(8,128)(2,1)S(1)} collective-permute-done((bf16[1,192,4096]{2,1,0:T(8,128)(2,1)S(1)}, bf16[1,192,4096]{2,1,0:T(8,128)(2,1)S(1)}, u32[]{:S(2)}, u32[]{:S(2)}) %collective-permute-start.1) | collective-permute-done | bytes 1572896 | tf_op jit(solution)/shard_map/ppermute | solution.py:14
  329.1 1.7 add_convert_fusion.2
  330.8 7.0 %all-to-all-start.3 = ((bf16[16,64,512]{2,1,0:T(8,128)(2,1)}), bf16[16,64,512]{2,1,0:T(8,128)(2,1)S(1)}, u32[]{:S(2)}, u32[]{:S(2)}) async-start(bf16[16,64,512]{2,1,0:T(8,128)(2,1)} %reduce-scatter.2.cloned.1.call-done), calls=%async_computation.4 | async-start | bytes 2097152 | tf_op jit(solution)/shard_map/all_to_all | solution.py:77
  337.8 5.3 %add_convert_fusion.1 = bf16[1,2,192,4096]{3,2,1,0:T(8,128)(2,1)} fusion(bf16[1,2,192,4096]{3,2,1,0:T(8,128)(2,1)} %collective-permute-done, bf16[1,1,192,4096]{3,2,1,0:T(8,128)(2,1)} %copy-done.4, bf16[1,1,192,4096]{3,2,1,0:T(8,128)(2,1)S(1)} %fusion), kind=kLoop, calls=%fused_computation.6 | loop fusion | flops 7864320 | bytes 9437184 | tf_op jit(solution)/shard_map/convert_element_type | solution.py:94
  343.1 11.2 %all-to-all-done.3 = bf16[16,64,512]{2,1,0:T(8,128)(2,1)S(1)} async-done(((bf16[16,64,512]{2,1,0:T(8,128)(2,1)}), bf16[16,64,512]{2,1,0:T(8,128)(2,1)S(1)}, u32[]{:S(2)}, u32[]{:S(2)}) %all-to-all-start.3) | async-done | bytes 1048608 | tf_op jit(solution)/shard_map/all_to_all | solution.py:77
  354.3 2.0 gather_fusion.3
  356.2 0.1 gather.21
  356.4 1.3 reduce_sum.25
  (25 shorter events, 0.1 us)
Async XLA Ops:
  7.2 178.2 %copy-start = (bf16[1,192,4096]{2,1,0:T(8,128)(2,1)S(1)}, bf16[1,192,4096]{2,1,0:T(8,128)(2,1)}, u32[]{:S(2)}) copy-start(bf16[1,192,4096]{2,1,0:T(8,128)(2,1)} %param.11) | copy-start | bytes 4718596
  7.2 12.6 %copy-start.2 = (bf16[128,512]{1,0:T(8,128)(2,1)S(1)}, bf16[128,512]{1,0:T(8,128)(2,1)}, u32[]{:S(2)}) copy-start(bf16[128,512]{1,0:T(8,128)(2,1)} %param.6) | copy-start | bytes 393220
  7.2 104.3 %all-gather.2.cloned.1.call-start = ((), (), s32[]{:S(2)}) async-start(), calls=%async_computation.5 | async-start | bytes 9437184 | tf_op jit(solution)/shard_map/all_gather | solution.py:49
  23.7 25.0 %copy-start.3 = (bf16[128,512]{1,0:T(8,128)(2,1)S(1)}, bf16[128,512]{1,0:T(8,128)(2,1)}, u32[]{:S(2)}) copy-start(bf16[128,512]{1,0:T(8,128)(2,1)} %param.7) | copy-start | bytes 393220
  78.5 106.8 %all-to-all-start.1 = ((bf16[8,1024,512]{1,2,0:T(8,128)(2,1)}), bf16[8,1024,512]{1,2,0:T(8,128)(2,1)}, u32[]{:S(2)}, u32[]{:S(2)}) async-start(bf16[8,1024,512]{1,2,0:T(8,128)(2,1)} %stack.12), calls=%async_computation.1 | async-start | bytes 16777216 | tf_op jit(solution)/shard_map/all_to_all | solution.py:51
  83.5 247.3 %reduce-scatter.2.cloned.1.call-start = ((), (), s32[]{:S(2)}) async-start(), calls=%async_computation.6 | async-start | bytes 9437184 | tf_op jit(solution)/shard_map/reduce_scatter | solution.py:71
  111.5 7.7 %copy-start.5 = (bf16[1,2,192,4096]{3,2,1,0:T(8,128)(2,1)S(1)}, bf16[1,2,192,4096]{3,2,1,0:T(8,128)(2,1)}, u32[]{:S(2)}) copy-start(bf16[1,2,192,4096]{3,2,1,0:T(8,128)(2,1)} %param.10) | copy-start | bytes 9437188
  111.5 7.7 %copy-start.7 = (bf16[1024,4096]{1,0:T(8,128)(2,1)S(1)}, bf16[1024,4096]{1,0:T(8,128)(2,1)}, u32[]{:S(2)}) copy-start(bf16[1024,4096]{1,0:T(8,128)(2,1)} %all-gather.2.cloned.1.call-done) | copy-start | bytes 25165828
  185.3 5.9 %copy-start.6 = (bf16[1,2,192,4096]{3,2,1,0:T(8,128)(2,1)S(1)}, bf16[1,2,192,4096]{3,2,1,0:T(8,128)(2,1)}, u32[]{:S(2)}) copy-start(bf16[1,2,192,4096]{3,2,1,0:T(8,128)(2,1)} %param.10) | copy-start | bytes 9437188
  221.5 2.3 copy-start.4
  221.5 5.2 %copy-start.8 = (f32[1024,192]{0,1:T(8,128)S(1)}, f32[1024,192]{0,1:T(8,128)}, u32[]{:S(2)}) copy-start(f32[1024,192]{0,1:T(8,128)} %fusion.6) | copy-start | bytes 2359300
  221.5 5.2 %copy-start.9 = (f32[1024,192]{0,1:T(8,128)S(1)}, f32[1024,192]{0,1:T(8,128)}, u32[]{:S(2)}) copy-start(f32[1024,192]{0,1:T(8,128)} %fusion.9) | copy-start | bytes 2359300
  223.7 114.0 %collective-permute-start = (bf16[1,2,192,4096]{3,2,1,0:T(8,128)(2,1)}, bf16[1,2,192,4096]{3,2,1,0:T(8,128)(2,1)}, u32[]{:S(2)}, u32[]{:S(2)}) collective-permute-start(bf16[1,2,192,4096]{3,2,1,0:T(8,128)(2,1)} %pad_maximum_fusion), channel_id=1, source_target_pairs={{0,64},{64,0},{8,72},{72,8},{16,80},{80,16},{24,88},{88,24},{32,96... | collective-permute-start | bytes 9437192 | tf_op jit(solution)/shard_map/ppermute | solution.py:14
  233.2 95.9 %collective-permute-start.1 = (bf16[1,192,4096]{2,1,0:T(8,128)(2,1)S(1)}, bf16[1,192,4096]{2,1,0:T(8,128)(2,1)S(1)}, u32[]{:S(2)}, u32[]{:S(2)}) collective-permute-start(bf16[1,192,4096]{2,1,0:T(8,128)(2,1)S(1)} %fusion.2), channel_id=1, source_target_pairs={{0,64},{64,0},{8,72},{72,8},{16,80},{80,16},{24,88},{88,24},{32,96... | collective-permute-start | bytes 4718600 | tf_op jit(solution)/shard_map/ppermute | solution.py:14
  330.8 23.5 %all-to-all-start.3 = ((bf16[16,64,512]{2,1,0:T(8,128)(2,1)}), bf16[16,64,512]{2,1,0:T(8,128)(2,1)S(1)}, u32[]{:S(2)}, u32[]{:S(2)}) async-start(bf16[16,64,512]{2,1,0:T(8,128)(2,1)} %reduce-scatter.2.cloned.1.call-done), calls=%async_computation.4 | async-start | bytes 2097152 | tf_op jit(solution)/shard_map/all_to_all | solution.py:77
  354.3 3.4 copy-start.1
Sparse Core Ops, SparseCore 0:
  48.8 62.6 all-gather.1
  210.9 52.4 reduce-scatter.1
